TPU v7x, 32 devices: a whole 2x2x4 slice. The times are simulated.
32 devices in a mesh: groups: 2 (over x), row: 16 (over z, y, core).
Axes of the slice: x: 2, y: 2, z: 4, core: 2. Of those that a mesh axis runs over, the one named last changes fastest.
Arguments:
- features: bfloat16 [64, 32, 4, 256], P('groups', 'row'), parts along dimension 0, may hold values from -6 to 6
- axial_taps: float32 [31, 256], replicated, may hold values from -1 to 1
- radial_taps: float32 [31, 256], replicated, may hold values from -1 to 1
- conv_bias: float32 [256], replicated, may hold values from -6 to 6
- ln_gain: float32 [256], replicated, may hold values from 0.5 to 1.5
- ln_bias: float32 [256], replicated, may hold values from -3 to 3
- w_in: bfloat16 [1024, 256], P('row'), may hold values from -0.375 to 0.375
- b_in: bfloat16 [1024], P('row'), may hold values from -3 to 3
- w_out: bfloat16 [1024, 256], P('row'), may hold values from -0.1875 to 0.1875
- b_out: float32 [256], replicated, may hold values from -1.75 to 1.75
- layer_scale: float32 [256], replicated, may hold values from 0.5 to 2
Outputs:
- block_out: bfloat16 [64, 32, 4, 256], P('groups', 'row'), parts along dimension 0
There are 2 independent parts, one for each index of `groups`. A program takes and returns all parts, laid end to end along the dimension named above; an argument that names none is the same for every part. Nothing has to cross between parts.
All inputs are finite; a program needn't handle non-finite values.
Results may differ from a plain program's by a relative error of at most 0.01.
Values may be sent and summed in bfloat16 or wider, within the bound.
A program may use at most 64 MiB of HBM per device.

v0:
```python
import functools

import jax
import jax.numpy as jnp
from jax import lax
from jax.experimental import pallas as pl
from jax.experimental.pallas import tpu as pltpu
from jax.sharding import PartitionSpec as P

MESH_ID = pl.DeviceIdType.MESH
F32 = jnp.float32
BF16 = jnp.bfloat16


def kernel(
    n, inner, taps, al, hl,
    x_ref, at_ref, rt_ref, cb_ref, lg_ref, lb_ref, wi_ref, bi_ref, wo_ref, bo_ref, ls_ref,
    o_ref,
    xpad, even, odd, send1, recv1, send2, recv2, wts, bias, normed,
    s1_sem, r1_sem, s2_sem, r2_sem, ws_sem, bs_sem, br_sem, wr_sem,
):
    channels = x_ref.shape[1]
    axial = x_ref.shape[0] // 8
    half = taps // 2
    per = channels // hl
    chips = n // 2
    me = lax.axis_index("row")
    grp = lax.axis_index("groups")
    core = lax.rem(me, 2)
    my_chip = lax.div(me, 2)
    sibling = me + 1 - 2 * core
    my_slot = core * chips + my_chip
    base = core * chips
    other = (1 - core) * chips
    outer = chips // inner
    my_z = lax.div(my_chip, inner)
    my_y = lax.rem(my_chip, inner)

    def to(d):
        return (grp, d)

    def ring(i, size, start):
        d = start + i
        return jnp.where(d >= size, d - size, d)

    barrier = pltpu.get_barrier_semaphore()

    def greet(i, c):
        pl.semaphore_signal(barrier, inc=1, device_id=to(ring(i, n, me)), device_id_type=MESH_ID)
        return c

    lax.fori_loop(1, n, greet, 0)
    pl.semaphore_signal(barrier, inc=1, device_id=(1 - grp, me), device_id_type=MESH_ID)

    wts[my_slot] = wi_ref[...]
    wts[n + my_slot] = wo_ref[...]
    unit = lax.broadcasted_iota(jnp.int32, (hl, channels), 0)
    lane = lax.broadcasted_iota(jnp.int32, (hl, channels), 1)
    place = (lane == unit + lax.rem(my_slot, per) * hl).astype(F32).astype(BF16)
    bias16 = jnp.broadcast_to(bi_ref[...].astype(F32), (16, hl)).astype(BF16)
    bias[my_slot] = jnp.dot(bias16, place, preferred_element_type=F32)[0:1]

    xpad[0:half] = jnp.zeros((half, 8, channels), F32)
    xpad[axial + half : axial + 2 * half] = jnp.zeros((half, 8, channels), F32)
    zeros8 = jnp.zeros((8, al, 8, channels), F32)
    even[0:8] = zeros8
    even[n + 8 : n + 16] = zeros8
    odd[0:8] = zeros8
    odd[n + 7 : n + 15] = zeros8
    odd[n + 15] = zeros8[0]

    def widen(i, c):
        rows = x_ref[pl.ds(pl.multiple_of(i * 64, 64), 64), :].astype(F32)
        xpad[pl.ds(half + i * 8, 8)] = rows.reshape(8, 8, channels)
        return c

    lax.fori_loop(0, axial // 8, widen, 0)

    def axial_chunk(i, c):
        acc = jnp.zeros((8, 8, channels), F32)
        for k in range(taps):
            acc = acc + xpad[pl.ds(i * 8 + k, 8)] * at_ref[k : k + 1, :][None]
        send1[pl.ds(i * 4, 4)] = acc.reshape(4, 16, channels).astype(BF16)
        return c

    lax.fori_loop(0, axial // 8, axial_chunk, 0)

    pl.semaphore_wait(barrier, n)

    def exchange1(i, c):
        d = ring(i, n, me)
        pltpu.make_async_remote_copy(
            src_ref=send1.at[d], dst_ref=recv1.at[me], send_sem=s1_sem, recv_sem=r1_sem,
            device_id=to(d), device_id_type=MESH_ID,
        ).start()
        return c

    lax.fori_loop(1, n, exchange1, 0)

    mine = grp * n
    theirs = (1 - grp) * n

    def piece_copy(piece, g, d):
        return pltpu.make_async_remote_copy(
            src_ref=wts.at[piece], dst_ref=wts.at[piece], send_sem=ws_sem,
            recv_sem=wr_sem.at[piece], device_id=(g, d), device_id_type=MESH_ID,
        )

    def chip_of(z, y):
        return z * inner + y

    def to_inner(piece):
        for j in range(1, inner):
            y = ring(j, inner, my_y)
            piece_copy(piece, grp, 2 * chip_of(my_z, y) + core).start()

    def own_outer(i, c):
        z = ring(i, outer, my_z)
        piece_copy(mine + my_slot, grp, 2 * chip_of(z, my_y) + core).start()
        return c

    lax.fori_loop(1, outer, own_outer, 0)
    to_inner(mine + my_slot)
    piece_copy(mine + my_slot, grp, sibling).start()
    piece_copy(theirs + my_slot, grp, sibling).start()

    def send_bias(i, c):
        d = ring(i, n, me)
        pltpu.make_async_remote_copy(
            src_ref=bias.at[my_slot], dst_ref=bias.at[my_slot], send_sem=bs_sem, recv_sem=br_sem,
            device_id=to(d), device_id_type=MESH_ID,
        ).start()
        return c

    lax.fori_loop(1, n, send_bias, 0)

    recv1[me] = send1[me]
    arrived = recv1.at[pl.ds(0, n - 1)]
    pltpu.make_async_copy(arrived, arrived, r1_sem).wait()

    def from_outer(i, c):
        piece = mine + base + chip_of(ring(i, outer, my_z), my_y)
        piece_copy(piece, grp, sibling).wait_recv()
        to_inner(piece)
        piece_copy(piece, 1 - grp, me).start()
        piece_copy(piece, grp, sibling).start()
        return c

    lax.fori_loop(1, outer, from_outer, 0)

    def pairs(s, c):
        v = recv1[s].astype(F32).reshape(al, 8, channels)
        even[s + 8] = v
        for a in range(al):
            odd[s + 8, a, 0:4, :] = v[a, 4:8]
            odd[s + 7, a, 4:8, :] = v[a, 0:4]
        return c

    lax.fori_loop(0, n, pairs, 0)

    def radial_chunk(i, c):
        p = i * 4
        acc = jnp.zeros((4, al, 8, channels), F32)
        for k in range(taps):
            shift = k - half
            if shift % 2 == 0:
                window = even[pl.ds(p + 8 + shift // 2, 4)]
            else:
                window = odd[pl.ds(p + 8 + (shift - 1) // 2, 4)]
            acc = acc + window * rt_ref[k : k + 1, :][None, None]
        acc = acc + cb_ref[...][None, None]
        send2[pl.ds(p, 4)] = acc.reshape(4, al * 8, channels).astype(BF16)
        return c

    lax.fori_loop(0, n // 4, radial_chunk, 0)

    def exchange2(i, c):
        d = ring(i, n, me)
        pltpu.make_async_remote_copy(
            src_ref=send2.at[d], dst_ref=recv2.at[me], send_sem=s2_sem, recv_sem=r2_sem,
            device_id=to(d), device_id_type=MESH_ID,
        ).start()
        return c

    lax.fori_loop(1, n, exchange2, 0)
    recv2[me] = send2[me]

    def from_inner(i, c):
        for j in range(1, inner):
            piece = mine + base + chip_of(ring(i, outer, my_z), ring(j, inner, my_y))
            piece_copy(piece, grp, sibling).wait_recv()
            piece_copy(piece, 1 - grp, me).start()
            piece_copy(piece, grp, sibling).start()
        return c

    lax.fori_loop(0, outer, from_inner, 0)

    def from_group(i, c):
        piece = theirs + base + ring(i, chips, my_chip)
        piece_copy(piece, grp, sibling).wait_recv()
        piece_copy(piece, grp, sibling).start()
        return c

    lax.fori_loop(1, chips, from_group, 0)

    arrived3 = bias.at[pl.ds(0, n - 1)]
    pltpu.make_async_copy(arrived3, arrived3, br_sem).wait()
    arrived2 = recv2.at[pl.ds(0, n - 1)]
    pltpu.make_async_copy(arrived2, arrived2, r2_sem).wait()

    block = min(16, n)
    rows = block * 16

    def norm(b, c):
        v = recv2[pl.ds(b * block, block)].reshape(rows, channels).astype(F32)
        average = jnp.mean(v, axis=-1, keepdims=True)
        centred = v - average
        variance = jnp.mean(centred * centred, axis=-1, keepdims=True)
        z = centred * lax.rsqrt(variance + 1e-06) * lg_ref[...] + lb_ref[...]
        normed[pl.ds(pl.multiple_of(b * rows, rows), rows), :] = z.astype(BF16)
        return c

    lax.fori_loop(0, n // block, norm, 0)

    def flat(w):
        if hl % 16:
            return w.astype(F32).reshape(per * hl, channels).astype(BF16)
        return w.reshape(per * hl, channels)

    def project(z, first):
        w_in = flat(wts[pl.ds(first, per)])
        w_out = flat(wts[pl.ds(n + first, per)])
        b_in = jnp.sum(bias[pl.ds(first, per)], axis=0)
        u = lax.dot_general(z, w_in, (((1,), (1,)), ((), ())), preferred_element_type=F32) + b_in
        g = 0.5 * u * (1.0 + jnp.tanh(0.7978845608028654 * (u + 0.044715 * (u * u * u))))
        return jnp.dot(g.astype(BF16), w_out, preferred_element_type=F32)

    def others(i, c):
        piece_copy(other + i, grp, sibling).wait_recv()
        piece_copy(n + other + i, grp, sibling).wait_recv()
        return c

    def mlp(b, c, late):
        at = pl.ds(pl.multiple_of(b * rows, rows), rows)
        z = normed[at, :]
        total = project(z, base)
        for g in range(1, chips // per):
            total = total + project(z, base + g * per)
        if late:
            lax.fori_loop(0, chips, others, 0)
        for g in range(chips // per):
            total = total + project(z, other + g * per)
        branch = (ls_ref[...] * (total + bo_ref[...])).astype(BF16)
        o_ref[at, :] = (x_ref[at, :].astype(F32) + branch.astype(F32)).astype(BF16)
        return c

    mlp(0, 0, True)
    if n // block > 1:
        lax.fori_loop(1, n // block, lambda b, c: mlp(b, c, False), 0)

    sent = send1.at[pl.ds(0, n - 1)]
    pltpu.make_async_copy(sent, sent, s1_sem).wait()
    sent2 = send2.at[pl.ds(0, n - 1)]
    pltpu.make_async_copy(sent2, sent2, s2_sem).wait()
    passed = wts.at[pl.ds(0, 2 * n - 2)]
    pltpu.make_async_copy(passed, passed, ws_sem).wait()
    pltpu.make_async_copy(arrived3, arrived3, bs_sem).wait()


def local(
    features,
    axial_taps,
    radial_taps,
    conv_bias,
    ln_gain,
    ln_bias,
    w_in,
    b_in,
    w_out,
    b_out,
    layer_scale,
    n,
    groups,
):
    axial, radial, theta, channels = features.shape
    taps = axial_taps.shape[0]
    hl = w_in.shape[0]
    al = axial // n
    inner = 1
    while 4 * inner * inner <= n // 2:
        inner *= 2
    assert groups == 2
    assert radial * theta == 8 and al == 2 and channels == 256 and taps == 31
    flat = features.reshape(axial * 8, channels)

    def row(v):
        return v.reshape(1, -1)

    vmem = pl.BlockSpec(memory_space=pltpu.VMEM)
    dma = pltpu.SemaphoreType.DMA
    out = pl.pallas_call(
        functools.partial(kernel, n, inner, taps, al, hl),
        out_shape=jax.ShapeDtypeStruct(flat.shape, BF16),
        in_specs=[vmem] * 11,
        out_specs=vmem,
        scratch_shapes=[
            pltpu.VMEM((axial + taps - 1, 8, channels), F32),
            pltpu.VMEM((n + 16, al, 8, channels), F32),
            pltpu.VMEM((n + 16, al, 8, channels), F32),
            pltpu.VMEM((n, 16, channels), BF16),
            pltpu.VMEM((n, 16, channels), BF16),
            pltpu.VMEM((n, 16, channels), BF16),
            pltpu.VMEM((n, 16, channels), BF16),
            pltpu.VMEM((2 * n, hl, channels), BF16),
            pltpu.VMEM((n, 1, channels), F32),
            pltpu.VMEM((axial * 8, channels), BF16),
            dma, dma, dma, dma, dma, dma, dma,
            dma((2 * n,)),
        ],
        compiler_params=pltpu.CompilerParams(
            collective_id=0, has_side_effects=True, vmem_limit_bytes=40 * 1024 * 1024
        ),
        cost_estimate=pl.CostEstimate(
            flops=axial * 8 * channels * 4 * (n * hl + taps),
            bytes_accessed=4 * axial * 8 * channels + 4 * n * hl * channels,
            transcendentals=axial * 8 * n * hl,
        ),
    )(
        flat, axial_taps, radial_taps, row(conv_bias), row(ln_gain), row(ln_bias),
        w_in, row(b_in), w_out, row(b_out), row(layer_scale),
    )
    return out.reshape(features.shape)


def solution(mesh):
    in_specs = (
        P("groups", "row", None, None),
        P(),
        P(),
        P(),
        P(),
        P(),
        P("row", None),
        P("row"),
        P("row", None),
        P(),
        P(),
    )
    out_specs = P("groups", "row", None, None)
    body = functools.partial(local, n=mesh.shape["row"], groups=mesh.shape["groups"])
    return jax.shard_map(body, mesh=mesh, in_specs=in_specs, out_specs=out_specs, check_vma=False)
```

profile of v0, /device:TPU:0, one launch (start us, length us, event | category | flops | bytes accessed | tf_op | source)
XLA Modules:
  0.0 22.9 jit_solution(14862056827421057499)
XLA Ops:
  0.0 0.0 copy-start
  0.0 0.0 copy-start.1
  0.0 0.0 copy-start.2
  0.0 0.0 copy-start.3
  0.0 0.0 copy-start.4
  0.0 0.0 copy-start.5
  0.0 0.0 copy-start.6
  0.0 0.0 copy-start.7
  0.0 0.0 copy-start.8
  0.1 0.0 copy-start.9
  0.1 1.0 %reshape.24.x_ref = bf16[256,256]{1,0:T(8,128)(2,1)S(1)} reshape(bf16[32,2,4,256]{3,2,1,0:T(4,128)(2,1)} %param.11) | data formatting | bytes 262144 | tf_op jit(solution)/shard_map/reshape | solution.py:294
  1.1 0.0 copy-done
  1.1 0.0 copy-done.1
  1.1 0.0 copy-done.2
  1.1 0.0 copy-done.3
  1.1 0.0 copy-done.4
  1.1 0.0 copy-done.5
  1.2 0.0 copy-done.6
  1.2 0.0 copy-done.7
  1.2 0.0 copy-done.8
  1.2 0.0 copy-done.9
  1.2 21.0 %shard_map.109 = bf16[256,256]{1,0:T(8,128)(2,1)S(1)} custom-call(bf16[256,256]{1,0:T(8,128)(2,1)S(1)} %reshape.24.x_ref, f32[31,256]{1,0:T(8,128)S(1)} %copy-done, f32[31,256]{1,0:T(8,128)S(1)} %copy-done.1, f32[1,256]{1,0:T(1,128)S(1)} %bitcast.6, f32[1,256]{1,0:T(1,128)S(1)} %bitcast.7, f32[1,256]{1,0:T(1,128)S(1)} %bitcast.8, ...), custom_call_target="tpu_custom_call" | custom-call | flops 276561920 | bytes 1310720 | tf_op jit(solution)/shard_map/pallas_call | solution.py:301
  22.2 0.7 %reshape.31 = bf16[32,2,4,256]{3,2,1,0:T(4,128)(2,1)} reshape(bf16[256,256]{1,0:T(8,128)(2,1)S(1)} %shard_map.109) | data formatting | bytes 262144 | tf_op jit(solution)/shard_map/reshape | solution.py:332
Async XLA Ops:
  0.0 1.1 %copy-start = (f32[31,256]{1,0:T(8,128)S(1)}, f32[31,256]{1,0:T(8,128)}, u32[]{:S(2)}) copy-start(f32[31,256]{1,0:T(8,128)} %at_ref.1) | copy-start | bytes 95236
  0.0 1.1 %copy-start.1 = (f32[31,256]{1,0:T(8,128)S(1)}, f32[31,256]{1,0:T(8,128)}, u32[]{:S(2)}) copy-start(f32[31,256]{1,0:T(8,128)} %rt_ref.1) | copy-start | bytes 95236
  0.0 1.1 %copy-start.2 = (bf16[64,256]{1,0:T(8,128)(2,1)S(1)}, bf16[64,256]{1,0:T(8,128)(2,1)}, u32[]{:S(2)}) copy-start(bf16[64,256]{1,0:T(8,128)(2,1)} %wi_ref.1) | copy-start | bytes 98308
  0.0 1.1 %copy-start.3 = (bf16[64,256]{1,0:T(8,128)(2,1)S(1)}, bf16[64,256]{1,0:T(8,128)(2,1)}, u32[]{:S(2)}) copy-start(bf16[64,256]{1,0:T(8,128)(2,1)} %wo_ref.1) | copy-start | bytes 98308
  0.0 1.1 %copy-start.4 = (f32[256]{0:T(256)S(1)}, f32[256]{0:T(256)}, u32[]{:S(2)}) copy-start(f32[256]{0:T(256)} %param.14) | copy-start | bytes 3076
  0.0 1.1 %copy-start.5 = (f32[256]{0:T(256)S(1)}, f32[256]{0:T(256)}, u32[]{:S(2)}) copy-start(f32[256]{0:T(256)} %param.15) | copy-start | bytes 3076
  0.0 1.1 %copy-start.6 = (f32[256]{0:T(256)S(1)}, f32[256]{0:T(256)}, u32[]{:S(2)}) copy-start(f32[256]{0:T(256)} %param.16) | copy-start | bytes 3076
  0.0 1.1 %copy-start.7 = (f32[256]{0:T(256)S(1)}, f32[256]{0:T(256)}, u32[]{:S(2)}) copy-start(f32[256]{0:T(256)} %param.20) | copy-start | bytes 3076
  0.0 1.1 %copy-start.8 = (f32[256]{0:T(256)S(1)}, f32[256]{0:T(256)}, u32[]{:S(2)}) copy-start(f32[256]{0:T(256)} %param.21) | copy-start | bytes 3076
  0.1 1.1 %copy-start.9 = (bf16[64]{0:T(256)(128)(2,1)S(1)}, bf16[64]{0:T(256)(128)(2,1)}, u32[]{:S(2)}) copy-start(bf16[64]{0:T(256)(128)(2,1)} %param.18) | copy-start | bytes 388
where the time goes:
time: 23.2 us; the launch traced here: 22.9 us
  Pallas kernels  21 us (91%)
  local copies, waits for them, and re-layouts  1.76 us (8%)
    pallas_call x1, Pallas kernels, local(): pl.pallas_call(functools.partial(kernel, n, inner, taps, al, hl), out_sha...  21 us
    reshape x1, local copies, waits for them, and re-layouts, local(): flat = features.reshape(axial * 8, channels)  1.03 us
    reshape x1, local copies, waits for them, and re-layouts, local(): return out.reshape(features.shape)  0.69 us

commit v1 on v0

v1 whole, which is shorter than its diff:
```python
import functools

import jax
import jax.numpy as jnp
from jax import lax
from jax.experimental import pallas as pl
from jax.experimental.pallas import tpu as pltpu
from jax.sharding import PartitionSpec as P

MESH_ID = pl.DeviceIdType.MESH
F32 = jnp.float32
BF16 = jnp.bfloat16


def swap_middle(first, second):
    top = lax.broadcasted_iota(jnp.int32, first.shape, first.ndim - 2) < 4
    axis = first.ndim - 2
    return (
        jnp.where(top, first, pltpu.roll(second, 4, axis)),
        jnp.where(top, pltpu.roll(first, 4, axis), second),
    )


def kernel(
    n, inner, taps, hl,
    x_ref, at_ref, rt_ref, cb_ref, lg_ref, lb_ref, wi_ref, bi_ref, wo_ref, bo_ref, ls_ref,
    o_ref,
    xb, atv, rtv, cbv, lgv, lbv, biv, bov, lsv,
    xpad, rpad, send1, recv1, send2, recv2, wts, bias,
    in_sem, up_sem, across_sem, s1_sem, r1_sem, s2_sem, r2_sem, ws_sem, wr_sem, bs_sem, br_sem,
):
    channels = x_ref.shape[3]
    axial = x_ref.shape[0]
    half = taps // 2
    per = channels // hl
    chips = n // 2
    outer = chips // inner
    q = 2 * inner
    me = lax.axis_index("row")
    grp = lax.axis_index("groups")
    core = lax.rem(me, 2)
    my_chip = lax.div(me, 2)
    my_z = lax.div(my_chip, inner)
    my_y = lax.rem(my_chip, inner)
    sibling = me + 1 - 2 * core
    base = core * chips
    my_slot = base + my_chip
    last = outer - 1
    mine = grp * n
    theirs = (1 - grp) * n

    def to(d):
        return (grp, d)

    def loop(lo, hi, body):
        def step(i, c):
            body(i)
            return c

        lax.fori_loop(lo, hi, step, 0)

    barrier = pltpu.get_barrier_semaphore()
    loop(me + 1, n, lambda d: pl.semaphore_signal(barrier, inc=1, device_id=to(d), device_id_type=MESH_ID))

    @pl.when(grp == 0)
    def _():
        pl.semaphore_signal(barrier, inc=1, device_id=(1, me), device_id_type=MESH_ID)

    pairs = (
        (wi_ref, wts.at[my_slot]), (wo_ref, wts.at[n + my_slot]), (bi_ref, biv), (x_ref, xb), (at_ref, atv), (rt_ref, rtv),
        (cb_ref, cbv), (lg_ref, lgv), (lb_ref, lbv), (bo_ref, bov), (ls_ref, lsv),
    )
    loads = [pltpu.make_async_copy(a, b, in_sem.at[i]) for i, (a, b) in enumerate(pairs)]
    for copy in loads:
        copy.start()

    @pl.when(me + grp > 0)
    def _():
        pl.semaphore_wait(barrier, me + grp)

    @pl.when(grp == 1)
    def _():
        pl.semaphore_signal(across_sem, inc=1, device_id=(0, me), device_id_type=MESH_ID)

    loop(0, me, lambda d: pl.semaphore_signal(up_sem.at[my_z], inc=1, device_id=to(d), device_id_type=MESH_ID))

    for copy in loads[:3]:
        copy.wait()
    unit = lax.broadcasted_iota(jnp.int32, (hl, channels), 0)
    lane = lax.broadcasted_iota(jnp.int32, (hl, channels), 1)
    place = (lane == unit + lax.rem(my_slot, per) * hl).astype(F32).astype(BF16)
    bias16 = jnp.broadcast_to(biv[...].astype(F32), (16, hl)).astype(BF16)
    bias[my_slot] = jnp.dot(bias16, place, preferred_element_type=F32)[0:1]

    def piece_copy(piece, g, d):
        return pltpu.make_async_remote_copy(
            src_ref=wts.at[piece], dst_ref=wts.at[piece], send_sem=ws_sem, recv_sem=wr_sem.at[piece],
            device_id=(g, d), device_id_type=MESH_ID,
        )

    def device(z, y):
        return 2 * (z * inner + y) + core

    def to_plane(z):
        @pl.when(my_z == last)
        def _():
            loop(0, inner, lambda j: piece_copy(mine + my_slot, grp, device(z, lax.rem(my_y + j, inner))).start())

        @pl.when(my_z != last)
        def _():
            piece_copy(mine + my_slot, grp, device(z, my_y)).start()

    def to_inner(piece):
        loop(1, inner, lambda j: piece_copy(piece, grp, device(my_z, lax.rem(my_y + j, inner))).start())

    @pl.when(my_z > 0)
    def _():
        to_plane(0)

    loads[3].wait()
    loads[4].wait()
    xpad[0:half] = jnp.zeros((half, 8, channels), F32)
    xpad[axial + half : axial + 2 * half] = jnp.zeros((half, 8, channels), F32)

    def widen(i):
        for j in range(8):
            for r in range(2):
                xpad[half + i * 8 + j, 4 * r : 4 * r + 4, :] = xb[i * 8 + j, r].astype(F32)

    loop(0, axial // 8, widen)

    def axial_chunk(i):
        acc = jnp.zeros((8, 8, channels), F32)
        for k in range(taps):
            acc = acc + xpad[pl.ds(i * 8 + k, 8)] * atv[k : k + 1, :][None]
        acc = acc.reshape(4, 2, 8, channels)
        low, high = swap_middle(acc[:, 0], acc[:, 1])
        send1[pl.ds(i * 4, 4)] = jnp.concatenate([low, high], axis=1).astype(BF16)

    loop(0, axial // 8, axial_chunk)

    def exchange1(d):
        pltpu.make_async_remote_copy(
            src_ref=send1.at[d], dst_ref=recv1.at[me], send_sem=s1_sem, recv_sem=r1_sem.at[my_z],
            device_id=to(d), device_id_type=MESH_ID,
        ).start()

    def send_bias(d):
        pltpu.make_async_remote_copy(
            src_ref=bias.at[my_slot], dst_ref=bias.at[my_slot], send_sem=bs_sem, recv_sem=br_sem,
            device_id=to(d), device_id_type=MESH_ID,
        ).start()

    loop(0, me, exchange1)
    pltpu.make_async_copy(send1.at[me], recv1.at[me], r1_sem.at[my_z]).start()
    loop(1, my_z, to_plane)
    loop(0, me, send_bias)

    def upward(z):
        behind = jnp.where(z == my_z, lax.rem(me, q), -1)

        @pl.when(behind < q - 1)
        def _():
            pl.semaphore_wait(up_sem.at[z], q - 1 - behind)

        loop(z * q + behind + 1, z * q + q, exchange1)

        @pl.when(z == my_z)
        def _():
            to_inner(mine + my_slot)
            piece_copy(mine + my_slot, grp, sibling).start()
            piece_copy(theirs + my_slot, grp, sibling).start()

        @pl.when(z != my_z)
        def _():
            to_plane(z)

        loop(z * q + behind + 1, z * q + q, send_bias)

    loop(my_z, outer, upward)

    @pl.when(grp == 0)
    def _():
        pl.semaphore_wait(across_sem, 1)

    def pass_on(piece):
        piece_copy(piece, 1 - grp, me).start()
        piece_copy(piece, grp, sibling).start()

    def from_line(z):
        piece = mine + base + z * inner + my_y
        piece_copy(piece, grp, sibling).wait_recv()

        @pl.when(z != last)
        def _():
            to_inner(piece)

        pass_on(piece)

    def from_inner(z):
        def step(j):
            piece = mine + base + z * inner + lax.rem(my_y + j, inner)
            piece_copy(piece, grp, sibling).wait_recv()
            pass_on(piece)

        loop(1, inner, step)

    def from_across(z):
        piece = theirs + base + z
        piece_copy(piece, grp, sibling).wait_recv()
        piece_copy(piece, grp, sibling).start()

    inside = my_z < last
    near = jnp.where(inside, my_z, 0)
    from_inner(my_z)
    loop(0, near, from_line)
    loop(my_z + 1, jnp.where(my_z == 0, outer, last), from_line)

    rpad[0:half] = jnp.zeros((half, 8, channels), F32)
    rpad[2 * n + half : 2 * n + 2 * half] = jnp.zeros((half, 8, channels), F32)
    loads[5].wait()
    loads[6].wait()

    def take(z):
        plane = recv1.at[pl.ds(z * q, q)]
        pltpu.make_async_copy(plane, plane, r1_sem.at[z]).wait()
        v = recv1[z * q : z * q + q].astype(F32)
        rpad[half + 2 * z * q : half + 2 * z * q + 2 * q] = v.reshape(2 * q, 8, channels)

    my_half = lax.div(me, n // 2)

    def exchange2(d):
        @pl.when(d != me)
        def _():
            pltpu.make_async_remote_copy(
                src_ref=send2.at[d], dst_ref=recv2.at[me], send_sem=s2_sem, recv_sem=r2_sem.at[my_half],
                device_id=to(d), device_id_type=MESH_ID,
            ).start()

        @pl.when(d == me)
        def _():
            pltpu.make_async_copy(send2.at[me], recv2.at[me], r2_sem.at[my_half]).start()

    def radial_chunk(i):
        acc = jnp.zeros((8, 8, channels), F32)
        for k in range(taps):
            acc = acc + rpad[pl.ds(i * 8 + k, 8)] * rtv[k : k + 1, :][None]
        acc = acc + cbv[...][None]
        send2[pl.ds(i * 4, 4)] = acc.reshape(4, 16, channels).astype(BF16)
        loop(i * 4, i * 4 + 4, exchange2)

    taken = 0
    for z in range(outer):
        need = min(outer, (q * z + q - 1 + 8) // q + 1)
        for p in range(taken, need):
            take(p)
        taken = need
        loop(z * q // 4, (z + 1) * q // 4, radial_chunk)

    loop(0, jnp.where(inside, 0, last), from_line)
    loop(jnp.where(inside & (my_z > 0), last, outer), outer, from_line)
    loop(jnp.where(inside, last, outer), outer, from_inner)
    loop(0, my_z, from_inner)
    loop(my_z + 1, last, from_inner)
    loop(1, chips, lambda i: from_across(lax.rem(my_chip + i, chips)))

    def from_sibling(i):
        piece_copy((1 - core) * chips + i, grp, sibling).wait_recv()
        piece_copy(n + (1 - core) * chips + i, grp, sibling).wait_recv()

    biases = bias.at[pl.ds(0, n - 1)]
    pltpu.make_async_copy(biases, biases, br_sem).wait()
    loop(0, chips, from_sibling)
    for copy in loads[7:]:
        copy.wait()

    block = min(8, n // 2)
    rows = block * 16

    def flat(w):
        if hl % 16:
            return w.astype(F32).reshape(per * hl, channels).astype(BF16)
        return w.reshape(per * hl, channels)

    def project(z, first):
        w_in = flat(wts[pl.ds(first, per)])
        w_out = flat(wts[pl.ds(n + first, per)])
        b_in = jnp.sum(bias[pl.ds(first, per)], axis=0)
        u = lax.dot_general(z, w_in, (((1,), (1,)), ((), ())), preferred_element_type=F32) + b_in
        g = 0.5 * u * (1.0 + jnp.tanh(0.7978845608028654 * (u + 0.044715 * (u * u * u))))
        return jnp.dot(g.astype(BF16), w_out, preferred_element_type=F32)

    def mlp(first):
        v = recv2[pl.ds(first, block)].reshape(rows, channels).astype(F32)
        average = jnp.mean(v, axis=-1, keepdims=True)
        centred = v - average
        variance = jnp.mean(centred * centred, axis=-1, keepdims=True)
        z = (centred * lax.rsqrt(variance + 1e-06) * lgv[...] + lbv[...]).astype(BF16)
        total = project(z, 0)
        for g in range(1, n // per):
            total = total + project(z, g * per)
        branch = (lsv[...] * (total + bov[...])).astype(BF16).astype(F32)
        branch = branch.reshape(block, 2, 8, channels)
        for a, part in enumerate(swap_middle(branch[:, 0], branch[:, 1])):
            for s in range(block):
                at = 2 * (first + s) + a
                v = xpad[half + at] + part[s]
                for r in range(2):
                    o_ref[at, r] = v[4 * r : 4 * r + 4].astype(BF16)

    upper = lax.div(my_z, (outer + 1) // 2)
    for b in range(2):
        h = jnp.where(upper == 0, b, 1 - b)
        part = recv2.at[pl.ds(0, n // 2)]
        pltpu.make_async_copy(part, part, r2_sem.at[h]).wait()
        loop(0, n // 2 // block, lambda i: mlp(h * (n // 2) + i * block))

    sent = send1.at[pl.ds(0, n - 1)]
    pltpu.make_async_copy(sent, sent, s1_sem).wait()
    sent2 = send2.at[pl.ds(0, n - 1)]
    pltpu.make_async_copy(sent2, sent2, s2_sem).wait()
    passed = wts.at[pl.ds(0, 2 * n - 1 - inner)]
    pltpu.make_async_copy(passed, passed, ws_sem).wait()

    @pl.when(my_z == last)
    def _():
        more = wts.at[pl.ds(0, outer * (inner - 1))]
        pltpu.make_async_copy(more, more, ws_sem).wait()

    pltpu.make_async_copy(biases, biases, bs_sem).wait()


def local(
    features,
    axial_taps,
    radial_taps,
    conv_bias,
    ln_gain,
    ln_bias,
    w_in,
    b_in,
    w_out,
    b_out,
    layer_scale,
    n,
    groups,
):
    axial, radial, theta, channels = features.shape
    taps = axial_taps.shape[0]
    hl = w_in.shape[0]
    inner = 1
    while 4 * inner * inner <= n // 2:
        inner *= 2
    assert groups == 2
    assert radial == 2 and theta == 4 and axial == 2 * n and channels == 256 and taps == 31

    def row(v):
        return v.reshape(1, -1)

    vmem = pl.BlockSpec(memory_space=pltpu.VMEM)
    hbm = pl.BlockSpec(memory_space=pltpu.HBM)
    dma = pltpu.SemaphoreType.DMA
    vec = pltpu.VMEM((1, channels), F32)
    return pl.pallas_call(
        functools.partial(kernel, n, inner, taps, hl),
        out_shape=pltpu.VMEM(features.shape, BF16),
        in_specs=[hbm] * 11,
        out_specs=vmem,
        scratch_shapes=[
            pltpu.VMEM(features.shape, BF16),
            pltpu.VMEM((taps, channels), F32),
            pltpu.VMEM((taps, channels), F32),
            vec, vec, vec,
            pltpu.VMEM((1, hl), BF16),
            vec, vec,
            pltpu.VMEM((axial + taps - 1, 8, channels), F32),
            pltpu.VMEM((2 * n + taps - 1, 8, channels), F32),
            pltpu.VMEM((n, 16, channels), BF16),
            pltpu.VMEM((n, 16, channels), BF16),
            pltpu.VMEM((n, 16, channels), BF16),
            pltpu.VMEM((n, 16, channels), BF16),
            pltpu.VMEM((2 * n, hl, channels), BF16),
            pltpu.VMEM((n, 1, channels), F32),
            dma((11,)),
            pltpu.SemaphoreType.REGULAR((n // 2 // inner,)),
            pltpu.SemaphoreType.REGULAR,
            dma, dma((n // 2 // inner,)), dma, dma((2,)), dma,
            dma((2 * n,)), dma, dma,
        ],
        compiler_params=pltpu.CompilerParams(
            collective_id=0, has_side_effects=True, vmem_limit_bytes=60 * 1024 * 1024
        ),
        cost_estimate=pl.CostEstimate(
            flops=axial * 8 * channels * 4 * (n * hl + taps),
            bytes_accessed=4 * axial * 8 * channels + 4 * n * hl * channels,
            transcendentals=axial * 8 * n * hl,
        ),
    )(
        features, axial_taps, radial_taps, row(conv_bias), row(ln_gain), row(ln_bias),
        w_in, row(b_in), w_out, row(b_out), row(layer_scale),
    )


def solution(mesh):
    in_specs = (
        P("groups", "row", None, None),
        P(),
        P(),
        P(),
        P(),
        P(),
        P("row", None),
        P("row"),
        P("row", None),
        P(),
        P(),
    )
    out_specs = P("groups", "row", None, None)
    body = functools.partial(local, n=mesh.shape["row"], groups=mesh.shape["groups"])
    return jax.shard_map(body, mesh=mesh, in_specs=in_specs, out_specs=out_specs, check_vma=False)
```

time: 23.2 us -> 23.8 us (1.026)
  the two profiles are of different devices: /device:TPU:0 before, /device:TPU:25 now
where the time goes in v1:
time: 23.8 us; the launch traced here: 23.7 us
  Pallas kernels  23 us (97%)
  local copies, waits for them, and re-layouts  0.66 us (3%)
    pallas_call x1, Pallas kernels, local(): pl.pallas_call(functools.partial(kernel, n, inner, taps, hl), out_shape=p...  23 us
    unnamed x1, local copies, waits for them, and re-layouts  0.66 us

profile of v1, /device:TPU:25, one launch (start us, length us, event | category | flops | bytes accessed | tf_op | source)
XLA Modules:
  0.0 23.7 jit_solution(16019808633322657977)
XLA Ops:
  0.0 23.0 %shard_map.109 = bf16[32,2,4,256]{3,2,1,0:T(4,128)(2,1)S(1)} custom-call(bf16[32,2,4,256]{3,2,1,0:T(4,128)(2,1)} %x_ref.1, f32[31,256]{1,0:T(8,128)} %at_ref.1, f32[31,256]{1,0:T(8,128)} %rt_ref.1, f32[1,256]{1,0:T(1,128)} %bitcast.6, f32[1,256]{1,0:T(1,128)} %bitcast.7, f32[1,256]{1,0:T(1,128)} %bitcast.8, bf16[64,256]{1,0:T(8,128)(2,1)} %wi_ref.1, ...), custom_call_target="tpu_custom_call" | custom-call | flops 276561920 | bytes 1310720 | tf_op jit(solution)/shard_map/pallas_call | solution.py:364
  23.0 0.7 %copy.13 = bf16[32,2,4,256]{3,2,1,0:T(4,128)(2,1)} copy(bf16[32,2,4,256]{3,2,1,0:T(4,128)(2,1)S(1)} %shard_map.109) | data formatting | bytes 262144

commit v2 on v1

--- a/solution.py
+++ b/solution.py
@@ -26,7 +26,7 @@
     x_ref, at_ref, rt_ref, cb_ref, lg_ref, lb_ref, wi_ref, bi_ref, wo_ref, bo_ref, ls_ref,
     o_ref,
     xb, atv, rtv, cbv, lgv, lbv, biv, bov, lsv,
-    xpad, rpad, send1, recv1, send2, recv2, wts, bias,
+    xpad, rpad, send1, recv1, send2, recv2, wts, bias, normed, sums,
     in_sem, up_sem, across_sem, s1_sem, r1_sem, s2_sem, r2_sem, ws_sem, wr_sem, bs_sem, br_sem,
 ):
     channels = x_ref.shape[3]
@@ -168,6 +168,7 @@
         @pl.when(z == my_z)
         def _():
             to_inner(mine + my_slot)
+            pl.when(core == 1)(lambda: to_inner(theirs + my_slot))
             piece_copy(mine + my_slot, grp, sibling).start()
             piece_copy(theirs + my_slot, grp, sibling).start()
 
@@ -201,20 +202,45 @@
         def step(j):
             piece = mine + base + z * inner + lax.rem(my_y + j, inner)
             piece_copy(piece, grp, sibling).wait_recv()
-            pass_on(piece)
+
+            @pl.when((core == 0) | ((z == last) & inside))
+            def _():
+                piece_copy(piece, 1 - grp, me).start()
+
+            piece_copy(piece, grp, sibling).start()
 
         loop(1, inner, step)
 
-    def from_across(z):
-        piece = theirs + base + z
+    def from_across(z, y):
+        piece = theirs + base + z * inner + y
         piece_copy(piece, grp, sibling).wait_recv()
+
+        @pl.when((core == 1) & (y == my_y) & (z != last))
+        def _():
+            to_inner(piece)
+
         piece_copy(piece, grp, sibling).start()
 
     inside = my_z < last
-    near = jnp.where(inside, my_z, 0)
-    from_inner(my_z)
-    loop(0, near, from_line)
-    loop(my_z + 1, jnp.where(my_z == 0, outer, last), from_line)
+
+    def nearest(visit):
+        def step(dist):
+            for z in (my_z - dist, my_z + dist):
+
+                @pl.when((z >= 0) & (z < outer))
+                def _(z=z):
+                    visit(z)
+
+        loop(1, outer, step)
+
+    def early(z):
+        return (inside & ((z < last) | (my_z == 0))) | ((my_z == last) & (z == last - 1))
+
+    @pl.when(inside)
+    def _():
+        from_inner(my_z)
+
+    nearest(lambda z: pl.when(early(z))(lambda: from_line(z)))
 
     rpad[0:half] = jnp.zeros((half, 8, channels), F32)
     rpad[2 * n + half : 2 * n + 2 * half] = jnp.zeros((half, 8, channels), F32)
@@ -257,25 +283,44 @@
         taken = need
         loop(z * q // 4, (z + 1) * q // 4, radial_chunk)
 
-    loop(0, jnp.where(inside, 0, last), from_line)
-    loop(jnp.where(inside & (my_z > 0), last, outer), outer, from_line)
-    loop(jnp.where(inside, last, outer), outer, from_inner)
-    loop(0, my_z, from_inner)
-    loop(my_z + 1, last, from_inner)
-    loop(1, chips, lambda i: from_across(lax.rem(my_chip + i, chips)))
-
-    def from_sibling(i):
-        piece_copy((1 - core) * chips + i, grp, sibling).wait_recv()
-        piece_copy(n + (1 - core) * chips + i, grp, sibling).wait_recv()
+
+    @pl.when(my_z == last)
+    def _():
+        from_inner(my_z)
+
+    nearest(lambda z: pl.when(jnp.logical_not(early(z)))(lambda: from_line(z)))
+    nearest(from_inner)
+
+    def across_inner(j):
+        y = lax.rem(my_y + j, inner)
+
+        @pl.when(j > 0)
+        def _():
+            from_across(my_z, y)
+
+        nearest(lambda z: from_across(z, y))
+
+    loop(0, inner, across_inner)
 
     biases = bias.at[pl.ds(0, n - 1)]
     pltpu.make_async_copy(biases, biases, br_sem).wait()
-    loop(0, chips, from_sibling)
     for copy in loads[7:]:
         copy.wait()
-
-    block = min(8, n // 2)
+    block = min(16, n)
     rows = block * 16
+
+    def norm(i):
+        v = recv2[pl.ds(i * block, block)].reshape(rows, channels).astype(F32)
+        average = jnp.mean(v, axis=-1, keepdims=True)
+        centred = v - average
+        variance = jnp.mean(centred * centred, axis=-1, keepdims=True)
+        z = centred * lax.rsqrt(variance + 1e-06) * lgv[...] + lbv[...]
+        normed[i] = z.astype(BF16)
+
+    for h in range(2):
+        part = recv2.at[pl.ds(0, n // 2)]
+        pltpu.make_async_copy(part, part, r2_sem.at[h]).wait()
+    loop(0, n // block, norm)
 
     def flat(w):
         if hl % 16:
@@ -290,30 +335,37 @@
         g = 0.5 * u * (1.0 + jnp.tanh(0.7978845608028654 * (u + 0.044715 * (u * u * u))))
         return jnp.dot(g.astype(BF16), w_out, preferred_element_type=F32)
 
-    def mlp(first):
-        v = recv2[pl.ds(first, block)].reshape(rows, channels).astype(F32)
-        average = jnp.mean(v, axis=-1, keepdims=True)
-        centred = v - average
-        variance = jnp.mean(centred * centred, axis=-1, keepdims=True)
-        z = (centred * lax.rsqrt(variance + 1e-06) * lgv[...] + lbv[...]).astype(BF16)
-        total = project(z, 0)
-        for g in range(1, n // per):
-            total = total + project(z, g * per)
+    def from_sibling(i):
+        piece_copy(i, grp, sibling).wait_recv()
+        piece_copy(n + i, grp, sibling).wait_recv()
+
+    def half_mlp(first):
+        def step(i):
+            total = project(normed[i], first)
+            for g in range(1, chips // per):
+                total = total + project(normed[i], first + g * per)
+            return total
+
+        return step
+
+    def own(i):
+        sums[i] = half_mlp(base)(i)
+
+    loop(0, n // block, own)
+    loop(chips - base, n - base, from_sibling)
+
+    def finish(i):
+        total = sums[i] + half_mlp(chips - base)(i)
         branch = (lsv[...] * (total + bov[...])).astype(BF16).astype(F32)
         branch = branch.reshape(block, 2, 8, channels)
         for a, part in enumerate(swap_middle(branch[:, 0], branch[:, 1])):
             for s in range(block):
-                at = 2 * (first + s) + a
+                at = 2 * (i * block + s) + a
                 v = xpad[half + at] + part[s]
                 for r in range(2):
                     o_ref[at, r] = v[4 * r : 4 * r + 4].astype(BF16)
 
-    upper = lax.div(my_z, (outer + 1) // 2)
-    for b in range(2):
-        h = jnp.where(upper == 0, b, 1 - b)
-        part = recv2.at[pl.ds(0, n // 2)]
-        pltpu.make_async_copy(part, part, r2_sem.at[h]).wait()
-        loop(0, n // 2 // block, lambda i: mlp(h * (n // 2) + i * block))
+    loop(0, n // block, finish)
 
     sent = send1.at[pl.ds(0, n - 1)]
     pltpu.make_async_copy(sent, sent, s1_sem).wait()
@@ -381,6 +433,8 @@
             pltpu.VMEM((n, 16, channels), BF16),
             pltpu.VMEM((2 * n, hl, channels), BF16),
             pltpu.VMEM((n, 1, channels), F32),
+            pltpu.VMEM((n // min(16, n), 16 * min(16, n), channels), BF16),
+            pltpu.VMEM((n // min(16, n), 16 * min(16, n), channels), F32),
             dma((11,)),
             pltpu.SemaphoreType.REGULAR((n // 2 // inner,)),
             pltpu.SemaphoreType.REGULAR,

time: 23.8 us -> 21.9 us (0.920)
  Pallas kernels: 23 us -> 21.1 us
    pallas_call x1, Pallas kernels: 23 us -> 21.1 us  [local(): pl.pallas_call(functools.partial(kernel, n, inner, taps, hl), out_shape=p...]
where the time goes in v2:
time: 21.9 us; the launch traced here: 21.8 us
  Pallas kernels  21.1 us (96%)
  local copies, waits for them, and re-layouts  0.66 us (3%)
    pallas_call x1, Pallas kernels, local(): pl.pallas_call(functools.partial(kernel, n, inner, taps, hl), out_shape=p...  21.1 us
    unnamed x1, local copies, waits for them, and re-layouts  0.66 us

profile of v2, /device:TPU:25, one launch (start us, length us, event | category | flops | bytes accessed | tf_op | source)
XLA Modules:
  0.0 21.8 jit_solution(16330873272520838643)
XLA Ops:
  0.0 21.1 %shard_map.109 = bf16[32,2,4,256]{3,2,1,0:T(4,128)(2,1)S(1)} custom-call(bf16[32,2,4,256]{3,2,1,0:T(4,128)(2,1)} %x_ref.1, f32[31,256]{1,0:T(8,128)} %at_ref.1, f32[31,256]{1,0:T(8,128)} %rt_ref.1, f32[1,256]{1,0:T(1,128)} %bitcast.6, f32[1,256]{1,0:T(1,128)} %bitcast.7, f32[1,256]{1,0:T(1,128)} %bitcast.8, bf16[64,256]{1,0:T(8,128)(2,1)} %wi_ref.1, ...), custom_call_target="tpu_custom_call" | custom-call | flops 276561920 | bytes 1310720 | tf_op jit(solution)/shard_map/pallas_call | solution.py:416
  21.1 0.7 %copy.13 = bf16[32,2,4,256]{3,2,1,0:T(4,128)(2,1)} copy(bf16[32,2,4,256]{3,2,1,0:T(4,128)(2,1)S(1)} %shard_map.109) | data formatting | bytes 262144

commit v3 on v2

--- a/solution.py
+++ b/solution.py
@@ -46,6 +46,7 @@
     base = core * chips
     my_slot = base + my_chip
     last = outer - 1
+    inside = my_z < last
     mine = grp * n
     theirs = (1 - grp) * n
 
@@ -67,8 +68,8 @@
         pl.semaphore_signal(barrier, inc=1, device_id=(1, me), device_id_type=MESH_ID)
 
     pairs = (
-        (wi_ref, wts.at[my_slot]), (wo_ref, wts.at[n + my_slot]), (bi_ref, biv), (x_ref, xb), (at_ref, atv), (rt_ref, rtv),
-        (cb_ref, cbv), (lg_ref, lgv), (lb_ref, lbv), (bo_ref, bov), (ls_ref, lsv),
+        (x_ref, xb), (at_ref, atv), (wi_ref, wts.at[my_slot]), (wo_ref, wts.at[n + my_slot]), (bi_ref, biv),
+        (rt_ref, rtv), (cb_ref, cbv), (lg_ref, lgv), (lb_ref, lbv), (bo_ref, bov), (ls_ref, lsv),
     )
     loads = [pltpu.make_async_copy(a, b, in_sem.at[i]) for i, (a, b) in enumerate(pairs)]
     for copy in loads:
@@ -83,14 +84,6 @@
         pl.semaphore_signal(across_sem, inc=1, device_id=(0, me), device_id_type=MESH_ID)
 
     loop(0, me, lambda d: pl.semaphore_signal(up_sem.at[my_z], inc=1, device_id=to(d), device_id_type=MESH_ID))
-
-    for copy in loads[:3]:
-        copy.wait()
-    unit = lax.broadcasted_iota(jnp.int32, (hl, channels), 0)
-    lane = lax.broadcasted_iota(jnp.int32, (hl, channels), 1)
-    place = (lane == unit + lax.rem(my_slot, per) * hl).astype(F32).astype(BF16)
-    bias16 = jnp.broadcast_to(biv[...].astype(F32), (16, hl)).astype(BF16)
-    bias[my_slot] = jnp.dot(bias16, place, preferred_element_type=F32)[0:1]
 
     def piece_copy(piece, g, d):
         return pltpu.make_async_remote_copy(
@@ -113,12 +106,24 @@
     def to_inner(piece):
         loop(1, inner, lambda j: piece_copy(piece, grp, device(my_z, lax.rem(my_y + j, inner))).start())
 
-    @pl.when(my_z > 0)
-    def _():
-        to_plane(0)
-
-    loads[3].wait()
-    loads[4].wait()
+    def first_to_plane(z):
+        def step(j):
+            for g, w_ref in enumerate((wi_ref, wo_ref)):
+
+                @pl.when(grp == g)
+                def _(w_ref=w_ref):
+                    pltpu.make_async_remote_copy(
+                        src_ref=w_ref, dst_ref=wts.at[mine + my_slot], send_sem=ws_sem,
+                        recv_sem=wr_sem.at[mine + my_slot],
+                        device_id=to(device(z, lax.rem(my_y + j, inner))), device_id_type=MESH_ID,
+                    ).start()
+
+        loop(0, jnp.where(my_z == last, inner, 1), step)
+
+    loop(0, jnp.minimum(my_z, 3), first_to_plane)
+
+    loads[0].wait()
+    loads[1].wait()
     xpad[0:half] = jnp.zeros((half, 8, channels), F32)
     xpad[axial + half : axial + 2 * half] = jnp.zeros((half, 8, channels), F32)
 
@@ -128,6 +133,12 @@
                 xpad[half + i * 8 + j, 4 * r : 4 * r + 4, :] = xb[i * 8 + j, r].astype(F32)
 
     loop(0, axial // 8, widen)
+
+    def exchange1(d):
+        pltpu.make_async_remote_copy(
+            src_ref=send1.at[d], dst_ref=recv1.at[me], send_sem=s1_sem, recv_sem=r1_sem.at[my_z],
+            device_id=to(d), device_id_type=MESH_ID,
+        ).start()
 
     def axial_chunk(i):
         acc = jnp.zeros((8, 8, channels), F32)
@@ -136,14 +147,17 @@
         acc = acc.reshape(4, 2, 8, channels)
         low, high = swap_middle(acc[:, 0], acc[:, 1])
         send1[pl.ds(i * 4, 4)] = jnp.concatenate([low, high], axis=1).astype(BF16)
+        loop(i * 4, jnp.minimum(i * 4 + 4, me), exchange1)
 
     loop(0, axial // 8, axial_chunk)
 
-    def exchange1(d):
-        pltpu.make_async_remote_copy(
-            src_ref=send1.at[d], dst_ref=recv1.at[me], send_sem=s1_sem, recv_sem=r1_sem.at[my_z],
-            device_id=to(d), device_id_type=MESH_ID,
-        ).start()
+    for copy in loads[2:5]:
+        copy.wait()
+    unit = lax.broadcasted_iota(jnp.int32, (hl, channels), 0)
+    lane = lax.broadcasted_iota(jnp.int32, (hl, channels), 1)
+    place = (lane == unit + lax.rem(my_slot, per) * hl).astype(F32).astype(BF16)
+    bias16 = jnp.broadcast_to(biv[...].astype(F32), (16, hl)).astype(BF16)
+    bias[my_slot] = jnp.dot(bias16, place, preferred_element_type=F32)[0:1]
 
     def send_bias(d):
         pltpu.make_async_remote_copy(
@@ -151,9 +165,8 @@
             device_id=to(d), device_id_type=MESH_ID,
         ).start()
 
-    loop(0, me, exchange1)
     pltpu.make_async_copy(send1.at[me], recv1.at[me], r1_sem.at[my_z]).start()
-    loop(1, my_z, to_plane)
+    loop(3, my_z, to_plane)
     loop(0, me, send_bias)
 
     def upward(z):
@@ -168,7 +181,7 @@
         @pl.when(z == my_z)
         def _():
             to_inner(mine + my_slot)
-            pl.when(core == 1)(lambda: to_inner(theirs + my_slot))
+            pl.when(my_z == last)(lambda: to_inner(theirs + my_slot))
             piece_copy(mine + my_slot, grp, sibling).start()
             piece_copy(theirs + my_slot, grp, sibling).start()
 
@@ -203,10 +216,7 @@
             piece = mine + base + z * inner + lax.rem(my_y + j, inner)
             piece_copy(piece, grp, sibling).wait_recv()
 
-            @pl.when((core == 0) | ((z == last) & inside))
-            def _():
-                piece_copy(piece, 1 - grp, me).start()
-
+            pl.when(inside)(lambda: piece_copy(piece, 1 - grp, me).start())
             piece_copy(piece, grp, sibling).start()
 
         loop(1, inner, step)
@@ -215,13 +225,8 @@
         piece = theirs + base + z * inner + y
         piece_copy(piece, grp, sibling).wait_recv()
 
-        @pl.when((core == 1) & (y == my_y) & (z != last))
-        def _():
-            to_inner(piece)
-
         piece_copy(piece, grp, sibling).start()
 
-    inside = my_z < last
 
     def nearest(visit):
         def step(dist):
@@ -233,14 +238,19 @@
 
         loop(1, outer, step)
 
-    def early(z):
-        return (inside & ((z < last) | (my_z == 0))) | ((my_z == last) & (z == last - 1))
-
     @pl.when(inside)
     def _():
         from_inner(my_z)
 
-    nearest(lambda z: pl.when(early(z))(lambda: from_line(z)))
+    loop(0, my_z, lambda i: pl.when(inside | (i < 1))(lambda: from_line(my_z - 1 - i)))
+    loop(my_z + 1, last, from_line)
+
+    @pl.when(inside)
+    def _():
+        loop(1, inner, lambda j: piece_copy(theirs + my_slot, grp, device(last, lax.rem(my_y + j, inner))).start())
+
+    pl.when(inside)(lambda: from_line(last))
+    nearest(lambda z: pl.when(inside & (z == last))(lambda: from_inner(z)))
 
     rpad[0:half] = jnp.zeros((half, 8, channels), F32)
     rpad[2 * n + half : 2 * n + 2 * half] = jnp.zeros((half, 8, channels), F32)
@@ -287,9 +297,9 @@
     @pl.when(my_z == last)
     def _():
         from_inner(my_z)
-
-    nearest(lambda z: pl.when(jnp.logical_not(early(z)))(lambda: from_line(z)))
-    nearest(from_inner)
+        loop(0, my_z, lambda i: pl.when(jnp.logical_not((i < 1)))(lambda: from_line(my_z - 1 - i)))
+
+    nearest(lambda z: pl.when(jnp.logical_not(inside & (z == last)))(lambda: from_inner(z)))
 
     def across_inner(j):
         y = lax.rem(my_y + j, inner)
@@ -371,14 +381,8 @@
     pltpu.make_async_copy(sent, sent, s1_sem).wait()
     sent2 = send2.at[pl.ds(0, n - 1)]
     pltpu.make_async_copy(sent2, sent2, s2_sem).wait()
-    passed = wts.at[pl.ds(0, 2 * n - 1 - inner)]
+    passed = wts.at[pl.ds(0, 2 * n - 2)]
     pltpu.make_async_copy(passed, passed, ws_sem).wait()
-
-    @pl.when(my_z == last)
-    def _():
-        more = wts.at[pl.ds(0, outer * (inner - 1))]
-        pltpu.make_async_copy(more, more, ws_sem).wait()
-
     pltpu.make_async_copy(biases, biases, bs_sem).wait()
 
 

time: 21.9 us -> 20.6 us (0.941)
  the two profiles are of different devices: /device:TPU:25 before, /device:TPU:0 now
where the time goes in v3:
time: 20.6 us; the launch traced here: 20.5 us
  Pallas kernels  19.8 us (96%)
  local copies, waits for them, and re-layouts  0.66 us (3%)
    pallas_call x1, Pallas kernels, local(): pl.pallas_call(functools.partial(kernel, n, inner, taps, hl), out_shape=p...  19.8 us
    unnamed x1, local copies, waits for them, and re-layouts  0.66 us

profile of v3, /device:TPU:0, one launch (start us, length us, event | category | flops | bytes accessed | tf_op | source)
XLA Modules:
  0.0 20.5 jit_solution(17638832452538411501)
XLA Ops:
  0.0 19.8 %shard_map.109 = bf16[32,2,4,256]{3,2,1,0:T(4,128)(2,1)S(1)} custom-call(bf16[32,2,4,256]{3,2,1,0:T(4,128)(2,1)} %x_ref.1, f32[31,256]{1,0:T(8,128)} %at_ref.1, f32[31,256]{1,0:T(8,128)} %rt_ref.1, f32[1,256]{1,0:T(1,128)} %bitcast.6, f32[1,256]{1,0:T(1,128)} %bitcast.7, f32[1,256]{1,0:T(1,128)} %bitcast.8, bf16[64,256]{1,0:T(8,128)(2,1)} %wi_ref.1, ...), custom_call_target="tpu_custom_call" | custom-call | flops 276561920 | bytes 1310720 | tf_op jit(solution)/shard_map/pallas_call | solution.py:420
  19.8 0.7 %copy.13 = bf16[32,2,4,256]{3,2,1,0:T(4,128)(2,1)} copy(bf16[32,2,4,256]{3,2,1,0:T(4,128)(2,1)S(1)} %shard_map.109) | data formatting | bytes 262144

commit v4 on v3

--- a/solution.py
+++ b/solution.py
@@ -185,13 +185,14 @@
             piece_copy(mine + my_slot, grp, sibling).start()
             piece_copy(theirs + my_slot, grp, sibling).start()
 
-        @pl.when(z != my_z)
+        @pl.when((z != my_z) & ((z < last) | (my_z == last - 1)))
         def _():
             to_plane(z)
 
         loop(z * q + behind + 1, z * q + q, send_bias)
 
-    loop(my_z, outer, upward)
+    loop(my_z, last, upward)
+    pl.when(jnp.logical_not(((my_z > 0) & (my_z < last - 1))))(lambda: upward(last))
 
     @pl.when(grp == 0)
     def _():
@@ -243,7 +244,9 @@
         from_inner(my_z)
 
     loop(0, my_z, lambda i: pl.when(inside | (i < 1))(lambda: from_line(my_z - 1 - i)))
+    pl.when(((my_z > 0) & (my_z < last - 1)))(lambda: upward(last))
     loop(my_z + 1, last, from_line)
+    pl.when(my_z < last - 1)(lambda: to_plane(last))
 
     @pl.when(inside)
     def _():

time: 20.6 us -> 19.9 us (0.966)
  Pallas kernels: 19.8 us -> 19 us
    pallas_call x1, Pallas kernels: 19.8 us -> 19 us  [local(): pl.pallas_call(functools.partial(kernel, n, inner, taps, hl), out_shape=p...]
where the time goes in v4:
time: 19.9 us; the launch traced here: 19.7 us
  Pallas kernels  19 us (95%)
  local copies, waits for them, and re-layouts  0.66 us (3%)
    pallas_call x1, Pallas kernels, local(): pl.pallas_call(functools.partial(kernel, n, inner, taps, hl), out_shape=p...  19 us
    unnamed x1, local copies, waits for them, and re-layouts  0.66 us

profile of v4, /device:TPU:0, one launch (start us, length us, event | category | flops | bytes accessed | tf_op | source)
XLA Modules:
  0.0 19.7 jit_solution(1075622340054722490)
XLA Ops:
  0.0 19.0 %shard_map.109 = bf16[32,2,4,256]{3,2,1,0:T(4,128)(2,1)S(1)} custom-call(bf16[32,2,4,256]{3,2,1,0:T(4,128)(2,1)} %x_ref.1, f32[31,256]{1,0:T(8,128)} %at_ref.1, f32[31,256]{1,0:T(8,128)} %rt_ref.1, f32[1,256]{1,0:T(1,128)} %bitcast.6, f32[1,256]{1,0:T(1,128)} %bitcast.7, f32[1,256]{1,0:T(1,128)} %bitcast.8, bf16[64,256]{1,0:T(8,128)(2,1)} %wi_ref.1, ...), custom_call_target="tpu_custom_call" | custom-call | flops 276561920 | bytes 1310720 | tf_op jit(solution)/shard_map/pallas_call | solution.py:423
  19.1 0.7 %copy.13 = bf16[32,2,4,256]{3,2,1,0:T(4,128)(2,1)} copy(bf16[32,2,4,256]{3,2,1,0:T(4,128)(2,1)S(1)} %shard_map.109) | data formatting | bytes 262144

commit v5 on v4

--- a/solution.py
+++ b/solution.py
@@ -167,7 +167,6 @@
 
     pltpu.make_async_copy(send1.at[me], recv1.at[me], r1_sem.at[my_z]).start()
     loop(3, my_z, to_plane)
-    loop(0, me, send_bias)
 
     def upward(z):
         behind = jnp.where(z == my_z, lax.rem(me, q), -1)
@@ -192,6 +191,7 @@
         loop(z * q + behind + 1, z * q + q, send_bias)
 
     loop(my_z, last, upward)
+    loop(0, me, send_bias)
     pl.when(jnp.logical_not(((my_z > 0) & (my_z < last - 1))))(lambda: upward(last))
 
     @pl.when(grp == 0)

time: 19.9 us -> 19.9 us (level)
  no operation moved by 1% of the time
where the time goes in v5:
time: 19.9 us; the launch traced here: 19.7 us
  Pallas kernels  19 us (95%)
  local copies, waits for them, and re-layouts  0.66 us (3%)
    pallas_call x1, Pallas kernels, local(): pl.pallas_call(functools.partial(kernel, n, inner, taps, hl), out_shape=p...  19 us
    unnamed x1, local copies, waits for them, and re-layouts  0.66 us

profile of v5, /device:TPU:0, one launch (start us, length us, event | category | flops | bytes accessed | tf_op | source)
XLA Modules:
  0.0 19.7 jit_solution(17738156262565271016)
XLA Ops:
  0.0 19.0 %shard_map.109 = bf16[32,2,4,256]{3,2,1,0:T(4,128)(2,1)S(1)} custom-call(bf16[32,2,4,256]{3,2,1,0:T(4,128)(2,1)} %x_ref.1, f32[31,256]{1,0:T(8,128)} %at_ref.1, f32[31,256]{1,0:T(8,128)} %rt_ref.1, f32[1,256]{1,0:T(1,128)} %bitcast.6, f32[1,256]{1,0:T(1,128)} %bitcast.7, f32[1,256]{1,0:T(1,128)} %bitcast.8, bf16[64,256]{1,0:T(8,128)(2,1)} %wi_ref.1, ...), custom_call_target="tpu_custom_call" | custom-call | flops 276561920 | bytes 1310720 | tf_op jit(solution)/shard_map/pallas_call | solution.py:423
  19.1 0.7 %copy.13 = bf16[32,2,4,256]{3,2,1,0:T(4,128)(2,1)} copy(bf16[32,2,4,256]{3,2,1,0:T(4,128)(2,1)S(1)} %shard_map.109) | data formatting | bytes 262144
